TPU v7x, 32 devices: a whole 2x2x4 slice. The times are simulated.
32 devices in a mesh: dom: 8 (over z, x), cls: 4 (over y, core).
Axes of the slice: x: 2, y: 2, z: 4, core: 2. Of those that a mesh axis runs over, the one named last changes fastest.
Arguments:
- images: bfloat16 [768, 13824], P('dom')
- pick_counts: int32 [8], replicated, may hold values from 0 to 96, as said below
- group_of: int32 [768], replicated, may hold values from 0 to 31
- ctf_table: float32 [32, 32], replicated, may hold values from -1 to 1
- precision: float32 [32], replicated, may hold values from 0.1 to 1
- references: bfloat16 [200, 13824], P('cls')
Outputs:
- new_refs: float32 [200, 13824], P('cls', 'dom')
- confidence: float32 [768], P('dom')
Inputs may be any that keep to these rules, and one draw needn't show every extreme that they name: `pick_counts`: the counts sum to 384; each reader and the reader half of the dom axis away hold 96 particles together, and some reader holds exactly 96.
All inputs are finite; a program needn't handle non-finite values.
Results may differ from a plain program's by a relative error of at most 0.0037.
Values may be sent and summed in bfloat16 or wider, within the bound.
A program may use at most 320 MiB of HBM per device.

v0:
```python
import math

import jax
import jax.numpy as jnp
from jax import lax
from jax.sharding import PartitionSpec as P

ROT = 36
CYCLES = 32
ANG = 216
STEP = 6
FEAT = 13824


ridge_term = 0.02


def merged(part, axis, combine):
    gathered = jax.tree.map(lambda a: lax.all_gather(a, axis), part)

    def take(source):
        return jax.tree.map(lambda a: lax.dynamic_index_in_dim(a, source, 0, False), gathered)

    return lax.fori_loop(
        1, lax.axis_size(axis), lambda source, state: combine(state, take(source)), take(0)
    )


def weigh_rows(pixels, groups, ctf_table, precision):
    onehot = (groups[:, None] == jnp.arange(ctf_table.shape[0], dtype=jnp.int32)[None, :]).astype(
        jnp.float32
    )
    ctf_rows = jnp.dot(onehot, ctf_table, precision=lax.Precision.HIGHEST)
    cycle_scale = precision[None, :] * ctf_rows
    ctf_power = precision[None, :] * jnp.square(ctf_rows)
    shaped = pixels.reshape(pixels.shape[0], CYCLES, 2 * ANG).astype(jnp.float32)
    weighted = (
        (cycle_scale[:, :, None] * shaped).astype(jnp.bfloat16).reshape(pixels.shape[0], FEAT)
    )
    return (weighted, ctf_power, onehot)


def combine_mass(earlier, later):
    highest = jnp.maximum(earlier[0], later[0])
    return (
        highest,
        earlier[1] * jnp.exp(earlier[0] - highest) + later[1] * jnp.exp(later[0] - highest),
    )


def class_work(weighted, ctf_power, onehot, references, valid_rows):
    rows_here = weighted.shape[0]
    classes = references.shape[0]
    shaped_refs = references.reshape(classes, CYCLES, 2 * ANG)
    energy = jnp.sum(jnp.square(shaped_refs.astype(jnp.float32)), axis=2)
    ref_power = jnp.dot(ctf_power, energy.T, precision=lax.Precision.HIGHEST)
    group_size = math.gcd(ROT, 6)
    pieces = []
    for block in range(ROT // group_size):
        rotated = jnp.concatenate(
            [
                jnp.roll(shaped_refs, 2 * (block * group_size + turn) * STEP, axis=2).reshape(
                    classes, FEAT
                )
                for turn in range(group_size)
            ],
            axis=0,
        )
        pieces.append(
            lax.dot_general(
                weighted, rotated, (((1,), (1,)), ((), ())), preferred_element_type=jnp.float32
            )
        )
    correlation = jnp.concatenate(pieces, axis=1).reshape(rows_here, ROT, classes)
    logits = correlation - 0.5 * ref_power[:, None, :]
    local_peak = jnp.max(logits, axis=(1, 2))
    local_mass = jnp.sum(jnp.exp(logits - local_peak[:, None, None]), axis=(1, 2))
    peak_logit, mass_total = merged((local_peak, local_mass), "cls", combine_mass)
    shifted = jnp.exp(logits - peak_logit[:, None, None])
    posterior = jnp.where(valid_rows[:, None, None], shifted / mass_total[:, None, None], 0.0)
    confidence = jnp.where(valid_rows, 1.0 / mass_total, 0.0)
    post_bf = posterior.astype(jnp.bfloat16)
    numerator = jnp.zeros((classes, CYCLES, 2 * ANG), jnp.float32)
    for block in range(ROT // group_size):
        chosen = post_bf[:, block * group_size : (block + 1) * group_size, :].reshape(
            rows_here, group_size * classes
        )
        partial_sum = lax.dot_general(
            chosen, weighted, (((0,), (0,)), ((), ())), preferred_element_type=jnp.float32
        )
        partial_sum = partial_sum.reshape(group_size, classes, CYCLES, 2 * ANG)
        for turn in range(group_size):
            numerator = numerator + jnp.roll(
                partial_sum[turn], -2 * (block * group_size + turn) * STEP, axis=2
            )
    weights = jnp.dot(jnp.sum(posterior, axis=1).T, onehot, precision=lax.Precision.HIGHEST)
    return (numerator.reshape(classes, FEAT), weights, confidence)


def body(images, pick_counts, group_of, ctf_table, precision, references):
    dom_count = lax.axis_size("dom")
    my_index = lax.axis_index("dom")
    read_slots = images.shape[0]
    per_owner = read_slots // dom_count
    own_rows = read_slots // 2
    ends_at = jnp.cumsum(pick_counts)
    starts = ends_at - pick_counts
    begin = starts[my_index]
    slot_grid = images.reshape(per_owner, dom_count, images.shape[1])
    outgoing = jnp.roll(slot_grid, begin % dom_count, axis=1)
    incoming = lax.all_to_all(outgoing, "dom", split_axis=1, concat_axis=1, tiled=True)
    order_rank = my_index + dom_count * jnp.arange(own_rows, dtype=jnp.int32)
    source = jnp.sum((ends_at[None, :] <= order_rank[:, None]).astype(jnp.int32), axis=1)
    position = order_rank - jnp.take(starts, source)
    flat_index = position // dom_count * dom_count + source
    pixels = jnp.take(incoming.reshape(per_owner * dom_count, images.shape[1]), flat_index, axis=0)
    groups = jnp.take(group_of, source * read_slots + position)
    weighted, ctf_power, onehot = weigh_rows(pixels, groups, ctf_table, precision)
    valid_rows = jnp.ones((own_rows,), bool)
    numerator, weights, owned_conf = class_work(weighted, ctf_power, onehot, references, valid_rows)
    offset = (my_index - starts[None, :]) % dom_count
    sent_slot = dom_count * jnp.arange(per_owner, dtype=jnp.int32)[:, None] + offset
    alive_mask = sent_slot < pick_counts[None, :]
    target = jnp.clip((starts[None, :] + sent_slot) // dom_count, 0, own_rows - 1)
    reply_grid = jnp.where(alive_mask, jnp.take(owned_conf, target), 0.0)
    returned = lax.all_to_all(reply_grid, "dom", split_axis=1, concat_axis=1, tiled=True)
    confidence = jnp.roll(returned, -(begin % dom_count), axis=1).reshape(read_slots)
    summed = lax.psum_scatter(numerator, "dom", scatter_dimension=1, tiled=True)
    weights_all = lax.psum(weights, "dom")
    denominator = precision[None, :] * jnp.dot(
        weights_all, jnp.square(ctf_table), precision=lax.Precision.HIGHEST
    )
    width = summed.shape[1]
    cycle_index = (my_index * width + jnp.arange(width, dtype=jnp.int32)) // (2 * ANG)
    spread = jnp.take(denominator, cycle_index, axis=1)
    new_refs = summed / (spread + ridge_term)
    return (new_refs, confidence)


def solution(mesh):
    return jax.shard_map(
        body,
        mesh=mesh,
        in_specs=(P("dom", None), P(), P(), P(), P(), P("cls", None)),
        out_specs=(P("cls", "dom"), P("dom")),
        check_vma=False,
    )
```

profile of v0, /device:TPU:0, one launch (start us, length us, event | category | flops | bytes accessed | tf_op | source)
XLA Modules:
  0.0 1461.6 jit_solution(17106278488559645978)
XLA Ops:
  18.1 7.4 all-to-all-start
  73.1 4.9 compare_and_fusion.1
  79.4 4.8 pad_maximum_fusion.35
  298.6 59.6 %concatenate.401 = bf16[300,13824]{1,0:T(8,128)(2,1)} concatenate(bf16[50,13824]{1,0:T(8,128)(2,1)} %param.13, bf16[50,13824]{1,0:T(8,128)(2,1)} %reshape.901, bf16[50,13824]{1,0:T(8,128)(2,1)} %reshape.902, bf16[50,13824]{1,0:T(8,128)(2,1)} %reshape.903, bf16[50,13824]{1,0:T(8,128)(2,1)} %reshape.904, bf16[50,13824]{1,0:T(8,128)(2,1)} %reshape.905), dimensions={0} | concatenate | bytes 16588800 | tf_op jit(solution)/shard_map/concatenate | solution.py:60
  358.2 56.2 %concatenate.408 = bf16[300,13824]{1,0:T(8,128)(2,1)} concatenate(bf16[50,13824]{1,0:T(8,128)(2,1)S(1)} %copy-done.53, bf16[50,13824]{1,0:T(8,128)(2,1)} %reshape.907, bf16[50,13824]{1,0:T(8,128)(2,1)} %reshape.908, bf16[50,13824]{1,0:T(8,128)(2,1)} %reshape.909, bf16[50,13824]{1,0:T(8,128)(2,1)} %reshape.910, bf16[50,13824]{1,0:T(8,128)(2,1)} %reshape.911), dimensions={0} | concatenate | bytes 16588800 | tf_op jit(solution)/shard_map/concatenate | solution.py:60
  414.4 59.7 %concatenate.415 = bf16[300,13824]{1,0:T(8,128)(2,1)} concatenate(bf16[50,13824]{1,0:T(8,128)(2,1)} %reshape.912, bf16[50,13824]{1,0:T(8,128)(2,1)} %reshape.913, bf16[50,13824]{1,0:T(8,128)(2,1)} %reshape.914, bf16[50,13824]{1,0:T(8,128)(2,1)} %reshape.915, bf16[50,13824]{1,0:T(8,128)(2,1)} %reshape.916, bf16[50,13824]{1,0:T(8,128)(2,1)} %reshape.917), dimensions={0} | concatenate | bytes 16588800 | tf_op jit(solution)/shard_map/concatenate | solution.py:60
  474.1 56.1 %concatenate.422 = bf16[300,13824]{1,0:T(8,128)(2,1)} concatenate(bf16[50,13824]{1,0:T(8,128)(2,1)S(1)} %copy-done.54, bf16[50,13824]{1,0:T(8,128)(2,1)} %reshape.919, bf16[50,13824]{1,0:T(8,128)(2,1)} %reshape.920, bf16[50,13824]{1,0:T(8,128)(2,1)} %reshape.921, bf16[50,13824]{1,0:T(8,128)(2,1)} %reshape.922, bf16[50,13824]{1,0:T(8,128)(2,1)} %reshape.923), dimensions={0} | concatenate | bytes 16588800 | tf_op jit(solution)/shard_map/concatenate | solution.py:60
  530.1 59.7 %concatenate.429 = bf16[300,13824]{1,0:T(8,128)(2,1)} concatenate(bf16[50,13824]{1,0:T(8,128)(2,1)} %reshape.924, bf16[50,13824]{1,0:T(8,128)(2,1)} %reshape.925, bf16[50,13824]{1,0:T(8,128)(2,1)} %reshape.926, bf16[50,13824]{1,0:T(8,128)(2,1)} %reshape.927, bf16[50,13824]{1,0:T(8,128)(2,1)} %reshape.928, bf16[50,13824]{1,0:T(8,128)(2,1)} %reshape.929), dimensions={0} | concatenate | bytes 16588800 | tf_op jit(solution)/shard_map/concatenate | solution.py:60
  589.8 56.3 %concatenate.436 = bf16[300,13824]{1,0:T(8,128)(2,1)} concatenate(bf16[50,13824]{1,0:T(8,128)(2,1)S(1)} %copy-done.55, bf16[50,13824]{1,0:T(8,128)(2,1)} %reshape.931, bf16[50,13824]{1,0:T(8,128)(2,1)} %reshape.932, bf16[50,13824]{1,0:T(8,128)(2,1)} %reshape.933, bf16[50,13824]{1,0:T(8,128)(2,1)} %reshape.934, bf16[50,13824]{1,0:T(8,128)(2,1)} %reshape.935), dimensions={0} | concatenate | bytes 16588800 | tf_op jit(solution)/shard_map/concatenate | solution.py:60
  655.2 5.9 fusion.99
  661.2 5.9 fusion.100
  667.2 5.9 fusion.101
  673.2 5.9 fusion.102
  679.2 5.9 fusion.103
  685.2 5.9 fusion.104
  694.4 6.7 all-reduce.2
  718.0 6.5 fusion.60
  748.6 6.5 fusion.59
  799.6 6.5 fusion.58
  826.6 4.9 squeeze.158
  844.3 6.4 fusion.57
  896.0 6.5 fusion.56
  909.6 4.7 squeeze.148
  937.9 5.9 squeeze.144
  950.5 5.7 fusion.55
  1057.4 5.0 concatenate.502
  1139.3 4.8 squeeze.156
  1185.6 5.0 concatenate.470
  1282.2 34.4 %add_add_fusion = f32[50,13824]{1,0:T(8,128)S(1)} fusion(f32[50,13824]{1,0:T(8,128)} %concatenate.514, f32[50,13824]{1,0:T(8,128)} %concatenate.512, f32[50,13824]{1,0:T(8,128)} %concatenate.510, f32[50,13824]{1,0:T(8,128)} %concatenate.508, f32[50,13824]{1,0:T(8,128)} %concatenate.506, f32[50,13824]{1,0:T(8,128)} %concatenate.504, ...), kind=kLoop, calls=%fused_computation.74 | loop fusion | flops 24192000 | bytes 102297600 | tf_op jit(solution)/shard_map/add | solution.py:93
  1324.2 5.7 all-to-all-start.1
  1330.1 40.0 %psum.7 = f32[50,32]{0,1:T(8,128)S(1)} all-reduce(f32[50,32]{0,1:T(8,128)S(1)} %fusion.27), channel_id=1, replica_groups=mesh['dom'=8,'cls'=4] {'dom'}, use_global_device_ids=true, to_apply=%region_9.10 | all-reduce | flops 1600 | bytes 12800 | tf_op jit(solution)/shard_map/psum | solution.py:129
  1374.4 77.6 %reduce-scatter.4.cloned.1.call-done = f32[1728,50]{1,0:T(8,128)} async-done(((f32[13824,50]{1,0:T(8,128)}), f32[1728,50]{1,0:T(8,128)}) %reduce-scatter.4.cloned.1.call-update) | async-done | bytes 345616
  (622 shorter events, 810.2 us)
Async XLA Ops:
  7.2 70.9 %copy-start = (s32[768]{0:T(1024)S(1)}, s32[768]{0:T(1024)}, u32[]{:S(2)}) copy-start(s32[768]{0:T(1024)} %param.10) | copy-start | bytes 9220
  9.3 8.8 copy-start.111
  18.1 7.6 copy-start.52
  18.1 628.7 %all-to-all-start = ((bf16[12,8,13824]{2,0,1:T(8,128)(2,1)}), bf16[12,8,13824]{2,0,1:T(8,128)(2,1)}, u32[]{:S(2)}, u32[]{:S(2)}) async-start(bf16[12,8,13824]{2,0,1:T(8,128)(2,1)} %copy.30), calls=%async_computation | async-start | bytes 7077888 | tf_op jit(solution)/shard_map/all_to_all | solution.py:111
  25.5 1426.5 %reduce-scatter.4.cloned.1.call-start = ((), (), s32[]{:S(2)}) async-start(), calls=%async_computation.3 | async-start | bytes 7962624
  69.8 9.0 copy-start.118
  69.8 9.0 copy-start.122
  79.3 4.8 copy-start.44
  79.4 4.8 copy-start.45
  79.4 4.8 copy-start.88
  79.4 4.8 copy-start.89
  289.2 8.2 copy-start.124
  298.6 59.6 %copy-start.53 = (bf16[50,13824]{1,0:T(8,128)(2,1)S(1)}, bf16[50,13824]{1,0:T(8,128)(2,1)}, u32[]{:S(2)}) copy-start(bf16[50,13824]{1,0:T(8,128)(2,1)} %reshape.906) | copy-start | bytes 4147204
  414.4 59.7 %copy-start.54 = (bf16[50,13824]{1,0:T(8,128)(2,1)S(1)}, bf16[50,13824]{1,0:T(8,128)(2,1)}, u32[]{:S(2)}) copy-start(bf16[50,13824]{1,0:T(8,128)(2,1)} %reshape.918) | copy-start | bytes 4147204
  530.1 59.7 %copy-start.55 = (bf16[50,13824]{1,0:T(8,128)(2,1)S(1)}, bf16[50,13824]{1,0:T(8,128)(2,1)}, u32[]{:S(2)}) copy-start(bf16[50,13824]{1,0:T(8,128)(2,1)} %reshape.930) | copy-start | bytes 4147204
  661.1 6.0 copy-start.104
  667.1 6.0 copy-start.105
  673.1 6.0 copy-start.106
  679.1 6.0 copy-start.107
  685.1 6.0 copy-start.108
  691.7 10.8 copy-start.34
  950.5 10.4 copy-start.2
  1057.4 5.0 slice-start.16
  1057.4 5.0 copy-start.77
  1096.4 4.7 slice-start.5
  1185.6 5.0 slice-start.9
  1322.0 7.8 copy-start.113
  1322.1 7.8 copy-start.121
  1322.1 48.1 %copy-start.119 = (f32[32]{0:T(128)S(1)}, f32[32]{0:T(128)}, u32[]{:S(2)}) copy-start(f32[32]{0:T(128)} %param.12) | copy-start | bytes 388
  1322.1 48.1 %copy-start.123 = (f32[32,32]{1,0:T(8,128)S(1)}, f32[32,32]{1,0:T(8,128)}, u32[]{:S(2)}) copy-start(f32[32,32]{1,0:T(8,128)} %param.11) | copy-start | bytes 12292
  1324.2 49.5 %all-to-all-start.1 = ((f32[12,8,1]{0,2,1:T(1,128)}), f32[12,8,1]{0,2,1:T(1,128)S(1)}, u32[]{:S(2)}, u32[]{:S(2)}) async-start(f32[12,8,1]{0,2,1:T(1,128)} %copy.33), calls=%async_computation.1 | async-start | bytes 8192 | tf_op jit(solution)/shard_map/all_to_all | solution.py:126
  1370.1 84.4 %copy-start.1 = (s32[768]{0:T(1024)S(1)}, s32[768]{0:T(1024)}, u32[]{:S(2)}) copy-start(s32[768]{0:T(1024)} %param.10) | copy-start | bytes 9220
  (128 other events, 424.7 us)
Sparse Core Ops, SparseCore 0:
  1321.2 130.7 reduce-scatter.3
where the time goes:
time: 1480 us; the launch traced here: 1460 us
  local copies, waits for them, and re-layouts  1040 us (70%)
  other arithmetic  212 us (14%)
  waiting for transfers between devices  77.6 us (5%)
  matrix products  56.9 us (4%)
  blocking collectives  46.7 us (3%)
  between operations  18.8 us (1%)
    concatenate x6, local copies, waits for them, and re-layouts, class_work(): jnp.concatenate([jnp.roll(shaped_refs, 2 * (block * group_size + turn) *...  347 us
    squeeze x35, local copies, waits for them, and re-layouts, class_work(): partial_sum[turn]  162 us
    concatenate x35, local copies, waits for them, and re-layouts, class_work(): jnp.roll(partial_sum[turn], -2 * (block * group_size + turn) * STEP, axis=2)  161 us
    reshape x35, local copies, waits for them, and re-layouts, class_work(): jnp.roll(shaped_refs, 2 * (block * group_size + turn) * STEP, axis=2)  151 us
    concatenate x35, other arithmetic, class_work(): jnp.roll(partial_sum[turn], -2 * (block * group_size + turn) * STEP, axis=2)  103 us
    unnamed x2, waiting for transfers between devices  77.6 us
    slice x98, local copies, waits for them, and re-layouts, class_work(): jnp.roll(partial_sum[turn], -2 * (block * group_size + turn) * STEP, axis=2)  67.1 us
    concatenate x18, other arithmetic, class_work(): jnp.roll(shaped_refs, 2 * (block * group_size + turn) * STEP, axis=2)  54.8 us
  transfers between devices with their start and end apart: 3, of which 1 were waited for; matrix products, arithmetic and copies ran while one was open for 43% of the time, Pallas kernels for 0%

commit v1 on v0

v1 whole, which is shorter than its diff:
```python
import functools

import jax
import jax.numpy as jnp
from jax import lax
from jax.experimental import pallas as pl
from jax.experimental.pallas import tpu as pltpu
from jax.sharding import PartitionSpec as P

CYCLES = 32
WIDE = 432
TURN = 12
FINE = 4
BLOCK = TURN * FINE
COARSE = WIDE // BLOCK
BUNCH = 8
DEPTH = CYCLES * BLOCK
SLOT = 64
ridge_term = 0.02
HIGH = lax.Precision.HIGHEST
f32 = jnp.float32
bf16 = jnp.bfloat16


def score_kernel(img, groups, ctf, precision, refs, twice, spread, stats, power, turned):
    rows = img.shape[0]
    classes = refs.shape[0]
    kinds = ctf.shape[0]
    group = groups[...]
    onehot = (group == lax.broadcasted_iota(jnp.int32, (rows, kinds), 1)).astype(f32)
    ctf_rows = jnp.dot(onehot, ctf[...], precision=HIGH, preferred_element_type=f32)
    prec = precision[...]
    scale = prec * ctf_rows
    ctf_power = prec * jnp.square(ctf_rows)
    power[...] = ctf_power

    fill = jnp.zeros((SLOT - classes, BUNCH * WIDE), bf16)
    energies = []
    for bunch in range(CYCLES // BUNCH):
        lanes = slice(bunch * BUNCH * WIDE, (bunch + 1) * BUNCH * WIDE)
        out = slice(bunch * BUNCH * BLOCK, (bunch + 1) * BUNCH * BLOCK)
        factor = jnp.concatenate(
            [
                jnp.broadcast_to(scale[:, c : c + 1], (rows, BLOCK))
                for c in range(bunch * BUNCH, (bunch + 1) * BUNCH)
            ],
            axis=1,
        )
        pixels = img[:, lanes]
        for s in range(COARSE):
            piece = jnp.concatenate(
                [
                    pixels[:, c * WIDE + s * BLOCK : c * WIDE + (s + 1) * BLOCK]
                    for c in range(BUNCH)
                ],
                axis=1,
            )
            value = (piece.astype(f32) * factor).astype(bf16)
            twice[s * rows : (s + 1) * rows, out] = value
            if s < COARSE - 1:
                twice[(s + COARSE) * rows : (s + COARSE + 1) * rows, out] = value
        block = jnp.concatenate([refs[:, lanes], fill], axis=0)
        for c in range(BUNCH):
            one = block[:, c * WIDE : (c + 1) * WIDE].astype(f32)
            energies.append(jnp.sum(one * one, axis=1, keepdims=True))
        for s in range(COARSE):
            for turn in range(FINE):
                parts = []
                for c in range(BUNCH):
                    first = s * BLOCK - turn * TURN
                    base = c * WIDE
                    if first < 0:
                        parts.append(block[:, base + WIDE + first : base + WIDE])
                        parts.append(block[:, base : base + first + BLOCK])
                    else:
                        parts.append(block[:, base + first : base + first + BLOCK])
                turned[s, turn * SLOT : (turn + 1) * SLOT, out] = jnp.concatenate(parts, axis=1)

    energy = jnp.concatenate(energies, axis=1)
    ref_power = lax.dot_general(
        ctf_power, energy, (((1,), (1,)), ((), ())), precision=HIGH, preferred_element_type=f32
    )
    half = 0.5 * jnp.concatenate([ref_power] * FINE, axis=1)

    spread[...] = jnp.zeros_like(spread)

    @pl.loop(0, COARSE)
    def _(s):
        start = pl.multiple_of(s * rows, 16)
        spread[...] += lax.dot_general(
            twice[pl.ds(start, COARSE * rows), :],
            turned[s],
            (((1,), (1,)), ((), ())),
            preferred_element_type=f32,
        )

    real = lax.broadcasted_iota(jnp.int32, (rows, FINE * SLOT), 1) % SLOT < classes
    highest = jnp.full((rows, FINE * SLOT), -jnp.inf, f32)
    for g in range(COARSE):
        part = slice(g * rows, (g + 1) * rows)
        logits = jnp.where(real, spread[part, :] - half, -jnp.inf)
        spread[part, :] = logits
        highest = jnp.maximum(highest, logits)
    peak = jnp.max(highest, axis=1, keepdims=True)
    total = jnp.zeros((rows, FINE * SLOT), f32)
    for g in range(COARSE):
        part = slice(g * rows, (g + 1) * rows)
        raised = jnp.exp(spread[part, :] - peak)
        spread[part, :] = raised
        total = total + raised
    mass = jnp.sum(total, axis=1, keepdims=True)
    lane = lax.broadcasted_iota(jnp.int32, (rows, 128), 1)
    stats[...] = jnp.where(lane == 0, peak, mass)


def sum_kernel(twice, spread, factor, power, out, chosen, sums):
    rows = factor.shape[0]
    parts, classes, width = out.shape
    share = CYCLES // parts
    times = factor[...]
    total = jnp.zeros((rows, FINE * SLOT), f32)
    for g in range(COARSE):
        part = slice(g * rows, (g + 1) * rows)
        posterior = spread[part, :] * times
        spread[part, :] = posterior
        total = total + posterior
    chosen[...] = spread[...].T.astype(bf16)
    weight = total[:, :SLOT]
    for turn in range(1, FINE):
        weight = weight + total[:, turn * SLOT : (turn + 1) * SLOT]
    denominator = jnp.dot(weight.T, power[...], precision=HIGH, preferred_element_type=f32)

    @pl.loop(0, COARSE)
    def _(s):
        start = pl.multiple_of(s * rows, 16)
        sums[s] = jnp.dot(
            chosen[...], twice[pl.ds(start, COARSE * rows), :], preferred_element_type=f32
        )

    place = lax.broadcasted_iota(jnp.int32, (SLOT, DEPTH), 1) % BLOCK

    def fold(s):
        kept = sums[s, :SLOT, :]
        over = jnp.zeros((SLOT, DEPTH), f32)
        for turn in range(1, FINE):
            moved = pltpu.roll(
                sums[s, turn * SLOT : (turn + 1) * SLOT, :], DEPTH - turn * TURN, 1
            )
            inside = place < BLOCK - turn * TURN
            kept = kept + jnp.where(inside, moved, 0.0)
            over = over + jnp.where(inside, 0.0, moved)
        return kept, pltpu.roll(over, BLOCK, 1)

    overs = []
    for s in range(COARSE):
        kept, over = fold(s)
        sums[s, :SLOT, :] = kept
        sums[s, SLOT : 2 * SLOT, :] = over
    upper = denominator.astype(bf16)
    lower = (denominator - upper.astype(f32)).astype(bf16)
    tail = jnp.zeros((SLOT, width - share * (WIDE + 2)), bf16)
    blocks = [
        (sums[s, :SLOT, :] + sums[(s + 1) % COARSE, SLOT : 2 * SLOT, :]).astype(bf16)
        for s in range(COARSE)
    ]
    for d in range(parts):
        pieces = [b[:, d * share * BLOCK : (d + 1) * share * BLOCK] for b in blocks]
        cycles = slice(d * share, (d + 1) * share)
        whole = jnp.concatenate(pieces + [upper[:, cycles], lower[:, cycles], tail], axis=1)
        out[d] = whole[:classes]


def finish_kernel(parts, out):
    count = parts.shape[0]
    share = out.shape[1] // WIDE
    total = parts[0].astype(f32)
    for d in range(1, count):
        total = total + parts[d].astype(f32)
    end = share * WIDE
    denominator = total[:, end : end + share] + total[:, end + share : end + 2 * share]
    cycles = []
    for c in range(share):
        numerator = jnp.concatenate(
            [
                total[:, (s * share + c) * BLOCK : (s * share + c + 1) * BLOCK]
                for s in range(COARSE)
            ],
            axis=1,
        )
        cycles.append(numerator / (denominator[:, c : c + 1] + ridge_term))
    out[...] = jnp.concatenate(cycles, axis=1)


def in_vmem(count):
    return [pl.BlockSpec(memory_space=pltpu.VMEM)] * count


def body(images, pick_counts, group_of, ctf_table, precision, references):
    dom_count = lax.axis_size("dom")
    me = lax.axis_index("dom")
    rows = images.shape[0]
    classes = references.shape[0]
    share = CYCLES // dom_count
    width = -(-share * (WIDE + 2) // 128) * 128
    slots = jnp.arange(rows, dtype=jnp.int32)
    alive = slots < lax.dynamic_index_in_dim(pick_counts, me, 0, False)
    groups = jnp.where(alive, lax.dynamic_slice_in_dim(group_of, me * rows, rows), -1)
    params = pltpu.CompilerParams(vmem_limit_bytes=56 * 2**20)
    twice, spread, stats, power = pl.pallas_call(
        score_kernel,
        out_shape=[
            jax.ShapeDtypeStruct(((2 * COARSE - 1) * rows, DEPTH), bf16),
            jax.ShapeDtypeStruct((COARSE * rows, FINE * SLOT), f32),
            jax.ShapeDtypeStruct((rows, 128), f32),
            jax.ShapeDtypeStruct((rows, CYCLES), f32),
        ],
        in_specs=in_vmem(5),
        out_specs=in_vmem(4),
        scratch_shapes=[pltpu.VMEM((COARSE, FINE * SLOT, DEPTH), bf16)],
        compiler_params=params,
        name="score",
    )(images, groups[:, None], ctf_table, precision[None, :], references)
    peak, mass = stats[:, 0], stats[:, 1]
    all_stats = lax.all_gather(stats[:, :2].T, "cls")
    top = jnp.max(all_stats[:, 0], axis=0)
    mass_total = jnp.sum(all_stats[:, 1] * jnp.exp(all_stats[:, 0] - top[None, :]), axis=0)
    confidence = jnp.where(alive, 1.0 / mass_total, 0.0)
    factor = jnp.where(alive, jnp.exp(peak - top) / mass_total, 0.0)
    partial = pl.pallas_call(
        sum_kernel,
        out_shape=jax.ShapeDtypeStruct((dom_count, classes, width), bf16),
        in_specs=in_vmem(4),
        out_specs=pl.BlockSpec(memory_space=pltpu.VMEM),
        scratch_shapes=[
            pltpu.VMEM((FINE * SLOT, COARSE * rows), bf16),
            pltpu.VMEM((COARSE, FINE * SLOT, DEPTH), f32),
        ],
        compiler_params=params,
        name="sums",
    )(twice, spread, factor[:, None], power)
    parts = lax.all_to_all(partial, "dom", split_axis=0, concat_axis=0, tiled=True)
    new_refs = pl.pallas_call(
        finish_kernel,
        out_shape=jax.ShapeDtypeStruct((classes, share * WIDE), f32),
        in_specs=in_vmem(1),
        out_specs=pl.BlockSpec(memory_space=pltpu.VMEM),
        compiler_params=params,
        name="finish",
    )(parts)
    return (new_refs, confidence)


def solution(mesh):
    return jax.shard_map(
        body,
        mesh=mesh,
        in_specs=(P("dom", None), P(), P(), P(), P(), P("cls", None)),
        out_specs=(P("cls", "dom"), P("dom")),
        check_vma=False,
    )
```

time: 1480 us -> 104 us (0.07); the launches traced: 1460 us -> 104 us
  local copies, waits for them, and re-layouts: 1040 us -> 4.28 us
  other arithmetic: 212 us -> 4.79 us
  matrix products: 56.9 us -> 0 us
  Pallas kernels: 0 us -> 44.4 us
  waiting for transfers between devices: 77.6 us -> 37 us
  blocking collectives: 46.7 us -> 6.19 us
  between operations: 18.8 us -> 0.65 us
    concatenate x49 -> x0, local copies, waits for them, and re-layouts: 512 us -> none  [the longest x6 347 us: class_work(): jnp.concatenate([jnp.roll(shaped_refs, 2 * (block * group_size + turn) *...]
    squeeze x35 -> x0, local copies, waits for them, and re-layouts: 162 us -> none  [class_work(): partial_sum[turn]]
    concatenate x55 -> x0, other arithmetic: 162 us -> none  [the longest x35 103 us: class_work(): jnp.roll(partial_sum[turn], -2 * (block * group_size + turn) * STEP, axis=2)]
    reshape x44 -> x0, local copies, waits for them, and re-layouts: 158 us -> none  [the longest x35 151 us: class_work(): jnp.roll(shaped_refs, 2 * (block * group_size + turn) * STEP, axis=2)]
    slice x140 -> x0, local copies, waits for them, and re-layouts: 154 us -> none  [the longest x98 67.1 us: class_work(): jnp.roll(partial_sum[turn], -2 * (block * group_size + turn) * STEP, axis=2)]
    unnamed x2 -> x0, waiting for transfers between devices: 77.6 us -> none
    dot_general x16 -> x0, matrix products: 56.9 us -> none  [the longest x6 35.2 us: class_work(): lax.dot_general(weighted, rotated, (((1,), (1,)), ((), ())), preferred_el...]
    pallas_call x0 -> x3, Pallas kernels: none -> 44.4 us  [the longest x1 23.6 us: body(): pl.pallas_call(score_kernel, out_shape=[jax.ShapeDtypeStruct(((2 * COARSE...]
  transfers between devices with their start and end apart: 3 -> 1, of which waited for: 1 -> 1; matrix products, arithmetic and copies ran while one was open for 43% -> 1% of each run, Pallas kernels for 0% -> 0%
where the time goes in v1:
time: 104 us
  Pallas kernels  44.4 us (43%)
  waiting for transfers between devices  37 us (36%)
  starting transfers between devices  6.33 us (6%)
  blocking collectives  6.19 us (6%)
  other arithmetic  4.79 us (5%)
  local copies, waits for them, and re-layouts  4.28 us (4%)
    all_to_all x1, waiting for transfers between devices, body(): lax.all_to_all(partial, 'dom', split_axis=0, concat_axis=0, tiled=True)  37 us
    pallas_call x1, Pallas kernels, body(): pl.pallas_call(score_kernel, out_shape=[jax.ShapeDtypeStruct(((2 * COARSE...  23.6 us
    pallas_call x1, Pallas kernels, body(): pl.pallas_call(sum_kernel, out_shape=jax.ShapeDtypeStruct((dom_count, cla...  18.1 us
    all_to_all x1, starting transfers between devices, body(): lax.all_to_all(partial, 'dom', split_axis=0, concat_axis=0, tiled=True)  6.33 us
    all_gather x1, blocking collectives, body(): all_stats = lax.all_gather(stats[:, :2].T, 'cls')  6.19 us
    pallas_call x1, Pallas kernels, body(): pl.pallas_call(finish_kernel, out_shape=jax.ShapeDtypeStruct((classes, sh...  2.7 us
    select_n x1, other arithmetic, body(): factor = jnp.where(alive, jnp.exp(peak - top) / mass_total, 0.0)  2.11 us
  transfers between devices with their start and end apart: 1, of which 1 were waited for; matrix products, arithmetic and copies ran while one was open for 1% of the time, Pallas kernels for 0%

profile of v1, /device:TPU:0, one launch (start us, length us, event | category | flops | bytes accessed | tf_op | source)
XLA Modules:
  0.0 103.6 jit_solution(10203828230249404288)
XLA Ops:
  0.6 1.3 %dynamic_slice.7 = s32[1]{0:T(128)} dynamic-slice(s32[8]{0:T(128)} %param.7, s32[]{:T(128)S(6)} %select_n.19), dynamic_slice_sizes={1} | dynamic-slice | bytes 12 | tf_op jit(solution)/shard_map/jit(dynamic_index_in_dim)/dynamic_slice | solution.py:206
  1.9 1.4 %fusion = s32[96,1]{0,1:T(1,128)S(1)} fusion(s32[768]{0:T(1024)} %param.8, s32[]{:T(128)S(6)} %select_n.20, s32[]{:T(128)} %bitcast), kind=kLoop, calls=%fused_computation.6 | loop fusion | flops 192 | bytes 776 | tf_op jit(solution)/shard_map/broadcast_in_dim | solution.py:222
  3.4 0.7 copy.18.groups
  4.1 23.6 %score.1 = (bf16[1632,1536]{1,0:T(8,128)(2,1)}, f32[864,256]{1,0:T(8,128)}, f32[96,128]{1,0:T(8,128)}, f32[96,32]{1,0:T(8,128)}) custom-call(bf16[96,13824]{1,0:T(8,128)(2,1)} %img.1, s32[96,1]{1,0:T(8,128)} %copy.18.groups, f32[32,32]{1,0:T(8,128)} %ctf.1, f32[1,32]{1,0:T(1,128)} %bitcast.16, bf16[50,13824]{1,0:T(8,128)(2,1)} %refs.1), custom_call_target="tpu_custom_call" | custom-call | tf_op jit(solution)/shard_map/score/pallas_call | solution.py:209
  27.7 0.8 slice_bitcast_fusion
  28.5 0.1 copy.19
  28.6 6.2 %all-gather.1 = f32[4,2,96]{2,1,0:T(2,128)S(1)} all-gather(f32[1,2,96]{2,1,0:T(2,128)S(1)} %copy.19), channel_id=2, replica_groups=mesh['dom'=8,'cls'=4] {'cls'}, dimensions={0}, use_global_device_ids=true | all-gather | bytes 3840 | tf_op jit(solution)/shard_map/all_gather | solution.py:224
  34.8 0.1 copy.21
  34.9 0.1 copy.20
  35.0 2.1 %divide_select_fusion.factor = f32[96,1]{1,0:T(8,128)} fusion(f32[96,1]{1,0:T(8,128)S(1)} %copy.21, f32[96,1]{1,0:T(8,128)S(1)} %copy.20, f32[96,128]{1,0:T(8,128)} %get-tuple-element.8, s32[]{:T(128)} %bitcast), kind=kLoop, calls=%fused_computation | loop fusion | flops 384 | bytes 1540 | tf_op jit(solution)/shard_map/jit(_where)/select_n | solution.py:228
  37.1 18.1 %sums.1 = bf16[8,50,1792]{2,1,0:T(8,128)(2,1)} custom-call(bf16[1632,1536]{1,0:T(8,128)(2,1)} %get-tuple-element.6.twice, f32[864,256]{1,0:T(8,128)} %get-tuple-element.7.spread, f32[96,1]{1,0:T(8,128)} %divide_select_fusion.factor, f32[96,32]{1,0:T(8,128)} %get-tuple-element.9.power), custom_call_target="tpu_custom_call" | custom-call | tf_op jit(solution)/shard_map/sums/pallas_call | solution.py:229
  55.2 6.3 %all-to-all-start = ((bf16[8,50,1792]{2,1,0:T(8,128)(2,1)}), bf16[8,50,1792]{2,1,0:T(8,128)(2,1)S(1)}, u32[]{:S(2)}, u32[]{:S(2)}) async-start(bf16[8,50,1792]{2,1,0:T(8,128)(2,1)} %sums.1), calls=%async_computation | async-start | bytes 3211264 | tf_op jit(solution)/shard_map/all_to_all | solution.py:241
  61.6 1.2 %compare_select_fusion = f32[96]{0:T(128)} fusion(f32[96]{0:T(128)S(1)} %multiply_reduce_fusion, s32[]{:T(128)} %bitcast), kind=kLoop, calls=%fused_computation.4 | loop fusion | flops 288 | bytes 772 | tf_op jit(solution)/shard_map/jit(_where)/select_n | solution.py:227
  62.7 37.0 %all-to-all-done.parts = bf16[8,50,1792]{2,1,0:T(8,128)(2,1)S(1)} async-done(((bf16[8,50,1792]{2,1,0:T(8,128)(2,1)}), bf16[8,50,1792]{2,1,0:T(8,128)(2,1)S(1)}, u32[]{:S(2)}, u32[]{:S(2)}) %all-to-all-start) | async-done | bytes 1433632 | tf_op jit(solution)/shard_map/all_to_all | solution.py:241
  99.7 0.0 copy-start
  99.7 1.2 %copy-done = bf16[8,50,1792]{2,1,0:T(8,128)(2,1)} copy-done((bf16[8,50,1792]{2,1,0:T(8,128)(2,1)}, bf16[8,50,1792]{2,1,0:T(8,128)(2,1)S(1)}, u32[]{:S(2)}) %copy-start) | copy-done | bytes 1433624
  100.9 2.7 %finish.1 = f32[50,1728]{1,0:T(8,128)} custom-call(bf16[8,50,1792]{2,1,0:T(8,128)(2,1)} %copy-done), custom_call_target="tpu_custom_call" | custom-call | tf_op jit(solution)/shard_map/finish/pallas_call | solution.py:242
  (2 shorter events, 0.0 us)
Async XLA Ops:
  55.2 44.5 %all-to-all-start = ((bf16[8,50,1792]{2,1,0:T(8,128)(2,1)}), bf16[8,50,1792]{2,1,0:T(8,128)(2,1)S(1)}, u32[]{:S(2)}, u32[]{:S(2)}) async-start(bf16[8,50,1792]{2,1,0:T(8,128)(2,1)} %sums.1), calls=%async_computation | async-start | bytes 3211264 | tf_op jit(solution)/shard_map/all_to_all | solution.py:241
  99.7 1.2 %copy-start = (bf16[8,50,1792]{2,1,0:T(8,128)(2,1)}, bf16[8,50,1792]{2,1,0:T(8,128)(2,1)S(1)}, u32[]{:S(2)}) copy-start(bf16[8,50,1792]{2,1,0:T(8,128)(2,1)S(1)} %all-to-all-done.parts) | copy-start | bytes 4300804

commit v2 on v1

v2 whole, which is shorter than its diff:
```python
import functools

import jax
import jax.numpy as jnp
from jax import lax
from jax.experimental import pallas as pl
from jax.experimental.pallas import tpu as pltpu
from jax.sharding import PartitionSpec as P

CYCLES = 32
WIDE = 432
TURN = 12
FINE = 4
BLOCK = TURN * FINE
COARSE = WIDE // BLOCK
BUNCH = 8
DEPTH = CYCLES * BLOCK
SLOT = 64
ridge_term = 0.02
HIGH = lax.Precision.HIGHEST
f32 = jnp.float32
bf16 = jnp.bfloat16

MESH = pl.DeviceIdType.MESH


def em_kernel(
    parts,
    quads,
    img,
    counts,
    group_rows,
    ctf,
    precision,
    refs,
    out,
    conf,
    twice,
    turned,
    spread,
    chosen,
    fresh,
    kept,
    over,
    first_over,
    mine,
    give,
    take,
    den_mine,
    den_take,
    pass_on,
    land,
    stat_send,
    stat_land,
    stat_ssem,
    stat_rsem,
    give_ssem,
    give_rsem,
    den_ssem,
    den_rsem,
    pass_ssem,
    pass_rsem,
):
    rows = img.shape[0]
    classes = refs.shape[0]
    kinds = ctf.shape[0]
    share = CYCLES // parts
    lines = parts // 2
    half_depth = DEPTH // 2
    me = lax.axis_index("dom")
    my_class = lax.axis_index("cls")
    low, high = lax.rem(me, 2), lax.div(me, 2)
    mate = me + 1 - 2 * low

    barrier = pltpu.get_barrier_semaphore()
    for step in range(1, quads):
        other = lax.rem(my_class + step, quads)
        pl.semaphore_signal(barrier, inc=1, device_id=(me, other), device_id_type=MESH)
    pl.semaphore_signal(barrier, inc=1, device_id=(mate, my_class), device_id_type=MESH)
    for step in range(1, lines):
        other = 2 * lax.rem(high + step, lines) + low
        pl.semaphore_signal(barrier, inc=1, device_id=(other, my_class), device_id_type=MESH)

    order = [
        (h * 2 + l) * share + c for l in range(2) for h in range(lines) for c in range(share)
    ]

    count_lane = lax.broadcasted_iota(jnp.int32, (1, parts), 1)
    count = jnp.sum(jnp.where(count_lane == me, counts[...], 0), axis=1, keepdims=True)
    alive = lax.broadcasted_iota(jnp.int32, (1, rows), 1) < count
    group_row = jnp.where(alive, group_rows[pl.ds(me, 1), :], -1).astype(f32)
    group = jnp.broadcast_to(group_row, (8, rows)).T[:, :1]
    kind = lax.broadcasted_iota(jnp.int32, (rows, kinds), 1).astype(f32)
    onehot = (group == kind).astype(f32)
    ctf_rows = jnp.dot(onehot, ctf[...], precision=HIGH, preferred_element_type=f32)
    prec = precision[...]
    scale = prec * ctf_rows
    ctf_power = prec * jnp.square(ctf_rows)

    fill = jnp.zeros((SLOT - classes, WIDE), bf16)
    energies = [None] * CYCLES
    for bunch in range(CYCLES // BUNCH):
        lane_out = slice(bunch * BUNCH * BLOCK, (bunch + 1) * BUNCH * BLOCK)
        names = order[bunch * BUNCH : (bunch + 1) * BUNCH]
        factor = jnp.concatenate(
            [jnp.broadcast_to(scale[:, c : c + 1], (rows, BLOCK)) for c in names], axis=1
        )
        pixels = [img[:, c * WIDE : (c + 1) * WIDE] for c in names]
        for s in range(COARSE):
            piece = jnp.concatenate([p[:, s * BLOCK : (s + 1) * BLOCK] for p in pixels], axis=1)
            value = (piece.astype(f32) * factor).astype(bf16)
            twice[s * rows : (s + 1) * rows, lane_out] = value
            if s < COARSE - 1:
                twice[(s + COARSE) * rows : (s + COARSE + 1) * rows, lane_out] = value
        block = [
            jnp.concatenate([refs[:, c * WIDE : (c + 1) * WIDE], fill], axis=0) for c in names
        ]
        for c, b in zip(names, block):
            wide = b.astype(f32)
            energies[c] = jnp.sum(wide * wide, axis=1, keepdims=True)
        for s in range(COARSE):
            for turn in range(FINE):
                pieces = []
                first = s * BLOCK - turn * TURN
                for b in block:
                    if first < 0:
                        pieces.append(b[:, WIDE + first :])
                        pieces.append(b[:, : first + BLOCK])
                    else:
                        pieces.append(b[:, first : first + BLOCK])
                turned[s, turn * SLOT : (turn + 1) * SLOT, lane_out] = jnp.concatenate(
                    pieces, axis=1
                )

    energy = jnp.concatenate(energies, axis=1)
    ref_power = lax.dot_general(
        ctf_power, energy, (((1,), (1,)), ((), ())), precision=HIGH, preferred_element_type=f32
    )
    half = 0.5 * jnp.concatenate([ref_power] * FINE, axis=1)

    spread[...] = jnp.zeros_like(spread)

    @pl.loop(0, COARSE)
    def _(s):
        start = pl.multiple_of(s * rows, 16)
        spread[...] += lax.dot_general(
            twice[pl.ds(start, COARSE * rows), :],
            turned[s],
            (((1,), (1,)), ((), ())),
            preferred_element_type=f32,
        )

    real = lax.broadcasted_iota(jnp.int32, (rows, FINE * SLOT), 1) % SLOT < classes
    highest = jnp.full((rows, FINE * SLOT), -jnp.inf, f32)
    for g in range(COARSE):
        part = slice(g * rows, (g + 1) * rows)
        logits = jnp.where(real, spread[part, :] - half, -jnp.inf)
        spread[part, :] = logits
        highest = jnp.maximum(highest, logits)
    peak = jnp.max(highest, axis=1, keepdims=True)
    total = jnp.zeros((rows, FINE * SLOT), f32)
    for g in range(COARSE):
        part = slice(g * rows, (g + 1) * rows)
        raised = jnp.exp(spread[part, :] - peak)
        spread[part, :] = raised
        total = total + raised
    mass = jnp.sum(total, axis=1, keepdims=True)
    lane = lax.broadcasted_iota(jnp.int32, (rows, 128), 1)
    stat_send[...] = jnp.where(lane == 0, peak, mass).T[:8, :]

    pl.semaphore_wait(barrier, quads - 1 + lines)
    stat_copies = []
    for step in range(1, quads):
        other = lax.rem(my_class + step, quads)
        copy = pltpu.make_async_remote_copy(
            src_ref=stat_send,
            dst_ref=stat_land.at[step - 1],
            send_sem=stat_ssem.at[step - 1],
            recv_sem=stat_rsem.at[step - 1],
            device_id=(me, other),
            device_id_type=MESH,
        )
        copy.start()
        stat_copies.append(copy)
    for copy in stat_copies:
        copy.wait()
    own_stat = stat_send[...]
    everyone = [own_stat] + [stat_land[i] for i in range(quads - 1)]
    top = everyone[0][:1]
    for stat in everyone[1:]:
        top = jnp.maximum(top, stat[:1])
    mass_total = jnp.zeros_like(top)
    for stat in everyone:
        mass_total = mass_total + stat[1:2] * jnp.exp(stat[:1] - top)
    conf[...] = jnp.where(alive, 1.0 / mass_total, 0.0)
    lower_by = jnp.where(alive, jnp.exp(own_stat[:1] - top) / mass_total, 0.0)
    times = jnp.broadcast_to(lower_by, (8, rows)).T[:, :1]

    total = jnp.zeros((rows, FINE * SLOT), f32)
    for g in range(COARSE):
        part = slice(g * rows, (g + 1) * rows)
        posterior = spread[part, :] * times
        spread[part, :] = posterior
        total = total + posterior
    chosen[...] = spread[...].T.astype(bf16)
    weight = total[:, :SLOT]
    for turn in range(1, FINE):
        weight = weight + total[:, turn * SLOT : (turn + 1) * SLOT]
    den = jnp.dot(weight.T, ctf_power, precision=HIGH, preferred_element_type=f32)
    den_mine[...] = jnp.concatenate([den, jnp.zeros((SLOT, 128 - CYCLES), f32)], axis=1)
    den_copy = pltpu.make_async_remote_copy(
        src_ref=den_mine,
        dst_ref=den_take,
        send_sem=den_ssem.at[0],
        recv_sem=den_rsem.at[0],
        device_id=(mate, my_class),
        device_id_type=MESH,
    )
    den_copy.start()

    place = lax.broadcasted_iota(jnp.int32, (SLOT, DEPTH), 1) % BLOCK

    def give_copy(s):
        return pltpu.make_async_remote_copy(
            src_ref=give.at[s],
            dst_ref=take.at[s],
            send_sem=give_ssem.at[s],
            recv_sem=give_rsem.at[s],
            device_id=(mate, my_class),
            device_id_type=MESH,
        )

    def emit(s, value):
        left, right = value[:classes, :half_depth], value[:classes, half_depth:]
        mine[s] = jnp.where(low == 0, left, right)
        give[s] = jnp.where(low == 0, right, left).astype(bf16)
        give_copy(s).start()

    def pass_copy(j, step):
        other = 2 * lax.rem(high + step, lines) + low
        return pltpu.make_async_remote_copy(
            src_ref=pass_on.at[j, step],
            dst_ref=land.at[j, step - 1],
            send_sem=pass_ssem.at[j, step - 1],
            recv_sem=pass_rsem.at[j, step - 1],
            device_id=(other, my_class),
            device_id_type=MESH,
        )

    wide_pair = pass_on.shape[-1]
    groups = [[s for s in (2 * j, 2 * j + 1) if s < COARSE] for j in range((COARSE + 1) // 2)]

    def forward(j):
        sums = []
        for s in groups[j]:
            give_copy(s).wait_recv()
            sums.append(mine[s] + take[s].astype(f32))
        last = j == len(groups) - 1
        if last:
            den_copy.wait_recv()
            den_all = den_mine[...] + den_take[...]
        for h in range(lines):
            pieces = [v[:, h * share * BLOCK : (h + 1) * share * BLOCK].astype(bf16) for v in sums]
            if last:
                near = den_all[:classes, 2 * h * share : (2 * h + 1) * share]
                far = den_all[:classes, (2 * h + 1) * share : (2 * h + 2) * share]
                some = jnp.where(low == 0, near, far)
                upper = some.astype(bf16)
                pieces += [upper, (some - upper.astype(f32)).astype(bf16)]
            used = sum(p.shape[1] for p in pieces)
            if used < wide_pair:
                pieces.append(jnp.zeros((classes, wide_pair - used), bf16))
            pass_on[j, lax.rem(h - high + lines, lines)] = jnp.concatenate(pieces, axis=1)
        for step in range(1, lines):
            pass_copy(j, step).start()

    for s in range(COARSE):

        @pl.loop(0, DEPTH // 384)
        def _(n):
            columns = pl.ds(pl.multiple_of(n * 384, 128), 384)
            fresh[:, columns] = jnp.dot(
                chosen[...],
                twice[s * rows : (s + COARSE) * rows, columns],
                preferred_element_type=f32,
            )

        stay = fresh[:SLOT, :]
        beyond = jnp.zeros((SLOT, DEPTH), f32)
        for turn in range(1, FINE):
            moved = pltpu.roll(fresh[turn * SLOT : (turn + 1) * SLOT, :], DEPTH - turn * TURN, 1)
            inside = place < BLOCK - turn * TURN
            stay = stay + jnp.where(inside, moved, 0.0)
            beyond = beyond + jnp.where(inside, 0.0, moved)
        beyond = pltpu.roll(beyond, BLOCK, 1)
        if s == 0:
            first_over[...] = beyond
        else:
            emit(s - 1, kept[...] + beyond)
        kept[...] = stay
        if s == COARSE - 1:
            emit(s, kept[...] + first_over[...])
        if s >= 4 and s % 2 == 0:
            forward(s // 2 - 2)
    for j in range(len(groups) - 2, len(groups)):
        forward(j)

    totals = []
    for j in range(len(groups)):
        value = pass_on[j, 0].astype(f32)
        for step in range(1, lines):
            pass_copy(j, step).wait_recv()
            value = value + land[j, step - 1].astype(f32)
        totals.append(value)
    end = share * BLOCK
    tail = totals[-1]
    den_sum = tail[:, end : end + share] + tail[:, end + share : end + 2 * share]
    cycles = []
    for c in range(share):
        numerator = jnp.concatenate(
            [
                totals[s // 2][
                    :, ((s % 2) * share + c) * BLOCK : ((s % 2) * share + c + 1) * BLOCK
                ]
                for s in range(COARSE)
            ],
            axis=1,
        )
        cycles.append(numerator / (den_sum[:, c : c + 1] + ridge_term))
    out[...] = jnp.concatenate(cycles, axis=1)

    den_copy.wait_send()
    for s in range(COARSE):
        give_copy(s).wait_send()
    for j in range(len(groups)):
        for step in range(1, lines):
            pass_copy(j, step).wait_send()


def body(images, pick_counts, group_of, ctf_table, precision, references):
    parts = lax.axis_size("dom")
    quads = lax.axis_size("cls")
    rows = images.shape[0]
    classes = references.shape[0]
    share = CYCLES // parts
    lines = parts // 2
    pairs = (COARSE + 1) // 2
    wide_pair = -(-max(2 * share * BLOCK, share * (BLOCK + 2)) // 128) * 128
    dma = pltpu.SemaphoreType.DMA
    new_refs, confidence = pl.pallas_call(
        functools.partial(em_kernel, parts, quads),
        out_shape=[
            jax.ShapeDtypeStruct((classes, share * WIDE), f32),
            jax.ShapeDtypeStruct((1, rows), f32),
        ],
        in_specs=[pl.BlockSpec(memory_space=pltpu.VMEM)] * 6,
        out_specs=[pl.BlockSpec(memory_space=pltpu.VMEM)] * 2,
        scratch_shapes=[
            pltpu.VMEM(((2 * COARSE - 1) * rows, DEPTH), bf16),
            pltpu.VMEM((COARSE, FINE * SLOT, DEPTH), bf16),
            pltpu.VMEM((COARSE * rows, FINE * SLOT), f32),
            pltpu.VMEM((FINE * SLOT, COARSE * rows), bf16),
            pltpu.VMEM((FINE * SLOT, DEPTH), f32),
            pltpu.VMEM((SLOT, DEPTH), f32),
            pltpu.VMEM((SLOT, DEPTH), f32),
            pltpu.VMEM((SLOT, DEPTH), f32),
            pltpu.VMEM((COARSE, classes, DEPTH // 2), f32),
            pltpu.VMEM((COARSE, classes, DEPTH // 2), bf16),
            pltpu.VMEM((COARSE, classes, DEPTH // 2), bf16),
            pltpu.VMEM((SLOT, 128), f32),
            pltpu.VMEM((SLOT, 128), f32),
            pltpu.VMEM((pairs, lines, classes, wide_pair), bf16),
            pltpu.VMEM((pairs, lines - 1, classes, wide_pair), bf16),
            pltpu.VMEM((8, rows), f32),
            pltpu.VMEM((quads - 1, 8, rows), f32),
            dma((quads - 1,)),
            dma((quads - 1,)),
            dma((COARSE,)),
            dma((COARSE,)),
            dma((1,)),
            dma((1,)),
            dma((pairs, lines - 1)),
            dma((pairs, lines - 1)),
        ],
        compiler_params=pltpu.CompilerParams(
            vmem_limit_bytes=56 * 2**20, collective_id=0, has_side_effects=True
        ),
        name="em",
    )(
        images,
        pick_counts[None, :],
        group_of.reshape(parts, rows),
        ctf_table,
        precision[None, :],
        references,
    )
    return (new_refs, confidence.reshape(rows))


def solution(mesh):
    return jax.shard_map(
        body,
        mesh=mesh,
        in_specs=(P("dom", None), P(), P(), P(), P(), P("cls", None)),
        out_specs=(P("cls", "dom"), P("dom")),
        check_vma=False,
    )
```

time: 104 us -> 69.3 us (0.67)
  waiting for transfers between devices: 37 us -> 0 us
  Pallas kernels: 44.4 us -> 64.1 us
  starting transfers between devices: 6.33 us -> 0 us
  blocking collectives: 6.19 us -> 0 us
  other arithmetic: 4.79 us -> 0 us
    all_to_all x1 -> x0, waiting for transfers between devices: 37 us -> none  [body(): lax.all_to_all(partial, 'dom', split_axis=0, concat_axis=0, tiled=True)]
    pallas_call x3 -> x1, Pallas kernels: 44.4 us -> 64.1 us  [body(): pl.pallas_call(functools.partial(em_kernel, parts, quads), out_shape=[jax...]
    all_to_all x1 -> x0, starting transfers between devices: 6.33 us -> none  [body(): lax.all_to_all(partial, 'dom', split_axis=0, concat_axis=0, tiled=True)]
    all_gather x1 -> x0, blocking collectives: 6.19 us -> none  [body(): all_stats = lax.all_gather(stats[:, :2].T, 'cls')]
    select_n x2 -> x0, other arithmetic: 3.3 us -> none  [the longest x1 2.11 us: body(): factor = jnp.where(alive, jnp.exp(peak - top) / mass_total, 0.0)]
    broadcast_in_dim x1 -> x0, other arithmetic: 1.43 us -> none  [body(): groups[:, None]]
    reshape x0 -> x1, local copies, waits for them, and re-layouts: none -> 1.35 us  [body(): group_of.reshape(parts, rows)]
    dynamic_slice x1 -> x0, local copies, waits for them, and re-layouts: 1.3 us -> none  [body(): alive = slots < lax.dynamic_index_in_dim(pick_counts, me, 0, False)]
  transfers between devices with their start and end apart: 1 -> 0, of which waited for: 1 -> 0; matrix products, arithmetic and copies ran while one was open for 1% -> 0% of each run, Pallas kernels for 0% -> 0%
where the time goes in v2:
time: 69.3 us; the launch traced here: 69.1 us
  Pallas kernels  64.1 us (92%)
  local copies, waits for them, and re-layouts  4.32 us (6%)
    pallas_call x1, Pallas kernels, body(): pl.pallas_call(functools.partial(em_kernel, parts, quads), out_shape=[jax...  64.1 us
    unnamed x2, local copies, waits for them, and re-layouts  2.97 us

profile of v2, /device:TPU:0, one launch (start us, length us, event | category | flops | bytes accessed | tf_op | source)
XLA Modules:
  0.0 69.1 jit_solution(16546913541845838834)
XLA Ops:
  0.6 1.4 %reshape.10.group_rows = s32[8,96]{1,0:T(8,128)} reshape(s32[768]{0:T(1024)} %param.8) | data formatting | bytes 6144 | tf_op jit(solution)/shard_map/reshape | solution.py:392
  2.0 64.1 %em.1 = (f32[50,1728]{1,0:T(8,128)}, f32[1,96]{1,0:T(1,128)}) custom-call(bf16[96,13824]{1,0:T(8,128)(2,1)} %img.1, s32[1,8]{1,0:T(1,128)} %bitcast.3, s32[8,96]{1,0:T(8,128)} %reshape.10.group_rows, f32[32,32]{1,0:T(8,128)} %ctf.1, f32[1,32]{1,0:T(1,128)} %bitcast.4, bf16[50,13824]{1,0:T(8,128)(2,1)} %refs.1), custom_call_target="tpu_custom_call" | custom-call | tf_op jit(solution)/shard_map/em/pallas_call | solution.py:350
  66.1 1.8 %copy.10 = f32[50,1728]{1,0:T(8,128)} copy(f32[50,1728]{1,0:T(8,128)} %get-tuple-element.8) | data formatting | bytes 691200
  67.9 1.2 %copy.11 = f32[96]{0:T(128)} copy(f32[96]{0:T(128)} %bitcast.5) | data formatting | bytes 768

commit v3 on v2

--- a/solution.py
+++ b/solution.py
@@ -88,7 +88,10 @@
     count_lane = lax.broadcasted_iota(jnp.int32, (1, parts), 1)
     count = jnp.sum(jnp.where(count_lane == me, counts[...], 0), axis=1, keepdims=True)
     alive = lax.broadcasted_iota(jnp.int32, (1, rows), 1) < count
-    group_row = jnp.where(alive, group_rows[pl.ds(me, 1), :], -1).astype(f32)
+    mine_row = group_rows[:, :rows]
+    for d in range(1, parts):
+        mine_row = jnp.where(me == d, group_rows[:, d * rows : (d + 1) * rows], mine_row)
+    group_row = jnp.where(alive, mine_row, -1).astype(f32)
     group = jnp.broadcast_to(group_row, (8, rows)).T[:, :1]
     kind = lax.broadcasted_iota(jnp.int32, (rows, kinds), 1).astype(f32)
     onehot = (group == kind).astype(f32)
@@ -97,58 +100,72 @@
     scale = prec * ctf_rows
     ctf_power = prec * jnp.square(ctf_rows)
 
-    fill = jnp.zeros((SLOT - classes, WIDE), bf16)
-    energies = [None] * CYCLES
-    for bunch in range(CYCLES // BUNCH):
-        lane_out = slice(bunch * BUNCH * BLOCK, (bunch + 1) * BUNCH * BLOCK)
-        names = order[bunch * BUNCH : (bunch + 1) * BUNCH]
+    def window(source, c):
+        begin = c * WIDE // 128 * 128
+        end = min(-(-(c + 1) * WIDE // 128) * 128, source.shape[1])
+        return source[:, begin:end], c * WIDE - begin
+
+    bunches = [order[i * BUNCH : (i + 1) * BUNCH] for i in range(CYCLES // BUNCH)]
+    for i, names in enumerate(bunches):
+        lane_out = slice(i * BUNCH * BLOCK, (i + 1) * BUNCH * BLOCK)
         factor = jnp.concatenate(
             [jnp.broadcast_to(scale[:, c : c + 1], (rows, BLOCK)) for c in names], axis=1
         )
-        pixels = [img[:, c * WIDE : (c + 1) * WIDE] for c in names]
+        pixels = [window(img, c) for c in names]
         for s in range(COARSE):
-            piece = jnp.concatenate([p[:, s * BLOCK : (s + 1) * BLOCK] for p in pixels], axis=1)
+            piece = jnp.concatenate(
+                [p[:, o + s * BLOCK : o + (s + 1) * BLOCK] for p, o in pixels], axis=1
+            )
             value = (piece.astype(f32) * factor).astype(bf16)
             twice[s * rows : (s + 1) * rows, lane_out] = value
             if s < COARSE - 1:
                 twice[(s + COARSE) * rows : (s + COARSE + 1) * rows, lane_out] = value
-        block = [
-            jnp.concatenate([refs[:, c * WIDE : (c + 1) * WIDE], fill], axis=0) for c in names
-        ]
-        for c, b in zip(names, block):
-            wide = b.astype(f32)
-            energies[c] = jnp.sum(wide * wide, axis=1, keepdims=True)
-        for s in range(COARSE):
+
+    fill = jnp.zeros((SLOT - classes, BUNCH * BLOCK), bf16)
+
+    def turn_refs(s):
+        for i, names in enumerate(bunches):
+            lane_out = slice(i * BUNCH * BLOCK, (i + 1) * BUNCH * BLOCK)
+            block = [window(refs, c) for c in names]
             for turn in range(FINE):
                 pieces = []
                 first = s * BLOCK - turn * TURN
-                for b in block:
+                for b, o in block:
                     if first < 0:
-                        pieces.append(b[:, WIDE + first :])
-                        pieces.append(b[:, : first + BLOCK])
+                        pieces.append(b[:, o + WIDE + first : o + WIDE])
+                        pieces.append(b[:, o : o + first + BLOCK])
                     else:
-                        pieces.append(b[:, first : first + BLOCK])
-                turned[s, turn * SLOT : (turn + 1) * SLOT, lane_out] = jnp.concatenate(
-                    pieces, axis=1
-                )
-
+                        pieces.append(b[:, o + first : o + first + BLOCK])
+                value = jnp.concatenate([jnp.concatenate(pieces, axis=1), fill], axis=0)
+                turned[s, turn * SLOT : (turn + 1) * SLOT, lane_out] = value
+
+    turn_refs(0)
+    for s in range(COARSE):
+        if s + 1 < COARSE:
+            turn_refs(s + 1)
+        product = lax.dot_general(
+            twice[s * rows : (s + COARSE) * rows, :],
+            turned[s],
+            (((1,), (1,)), ((), ())),
+            preferred_element_type=f32,
+        )
+        if s == 0:
+            spread[...] = product
+        else:
+            spread[...] += product
+
+    squares = jnp.zeros((SLOT, DEPTH), f32)
+    for s in range(COARSE):
+        wide = turned[s, :SLOT, :].astype(f32)
+        squares = squares + wide * wide
+    energies = [None] * CYCLES
+    for i, c in enumerate(order):
+        energies[c] = jnp.sum(squares[:, i * BLOCK : (i + 1) * BLOCK], axis=1, keepdims=True)
     energy = jnp.concatenate(energies, axis=1)
     ref_power = lax.dot_general(
         ctf_power, energy, (((1,), (1,)), ((), ())), precision=HIGH, preferred_element_type=f32
     )
     half = 0.5 * jnp.concatenate([ref_power] * FINE, axis=1)
-
-    spread[...] = jnp.zeros_like(spread)
-
-    @pl.loop(0, COARSE)
-    def _(s):
-        start = pl.multiple_of(s * rows, 16)
-        spread[...] += lax.dot_general(
-            twice[pl.ds(start, COARSE * rows), :],
-            turned[s],
-            (((1,), (1,)), ((), ())),
-            preferred_element_type=f32,
-        )
 
     real = lax.broadcasted_iota(jnp.int32, (rows, FINE * SLOT), 1) % SLOT < classes
     highest = jnp.full((rows, FINE * SLOT), -jnp.inf, f32)
@@ -217,8 +234,6 @@
         device_id_type=MESH,
     )
     den_copy.start()
-
-    place = lax.broadcasted_iota(jnp.int32, (SLOT, DEPTH), 1) % BLOCK
 
     def give_copy(s):
         return pltpu.make_async_remote_copy(
@@ -274,33 +289,42 @@
         for step in range(1, lines):
             pass_copy(j, step).start()
 
-    for s in range(COARSE):
-
-        @pl.loop(0, DEPTH // 384)
+    chunk = BUNCH * BLOCK
+    place = lax.broadcasted_iota(jnp.int32, (SLOT, chunk), 1) % BLOCK
+    for s in range(COARSE + 1):
+
+        @pl.loop(0, DEPTH // chunk)
         def _(n):
-            columns = pl.ds(pl.multiple_of(n * 384, 128), 384)
-            fresh[:, columns] = jnp.dot(
-                chosen[...],
-                twice[s * rows : (s + COARSE) * rows, columns],
-                preferred_element_type=f32,
-            )
-
-        stay = fresh[:SLOT, :]
-        beyond = jnp.zeros((SLOT, DEPTH), f32)
-        for turn in range(1, FINE):
-            moved = pltpu.roll(fresh[turn * SLOT : (turn + 1) * SLOT, :], DEPTH - turn * TURN, 1)
-            inside = place < BLOCK - turn * TURN
-            stay = stay + jnp.where(inside, moved, 0.0)
-            beyond = beyond + jnp.where(inside, 0.0, moved)
-        beyond = pltpu.roll(beyond, BLOCK, 1)
-        if s == 0:
-            first_over[...] = beyond
-        else:
-            emit(s - 1, kept[...] + beyond)
-        kept[...] = stay
-        if s == COARSE - 1:
-            emit(s, kept[...] + first_over[...])
-        if s >= 4 and s % 2 == 0:
+            columns = pl.ds(pl.multiple_of(n * chunk, 128), chunk)
+            if s > 0:
+                old = fresh.at[(s - 1) % 2]
+                stay = old[:SLOT, columns]
+                beyond = jnp.zeros((SLOT, chunk), f32)
+                for turn in range(1, FINE):
+                    moved = pltpu.roll(
+                        old[turn * SLOT : (turn + 1) * SLOT, columns], chunk - turn * TURN, 1
+                    )
+                    inside = place < BLOCK - turn * TURN
+                    stay = stay + jnp.where(inside, moved, 0.0)
+                    beyond = beyond + jnp.where(inside, 0.0, moved)
+                beyond = pltpu.roll(beyond, BLOCK, 1)
+                if s == 1:
+                    first_over[:, columns] = beyond
+                else:
+                    over[:, columns] = kept[:, columns] + beyond
+                kept[:, columns] = stay
+            if s < COARSE:
+                fresh[s % 2, :, columns] = jnp.dot(
+                    chosen[...],
+                    twice[s * rows : (s + COARSE) * rows, columns],
+                    preferred_element_type=f32,
+                )
+
+        if s > 1:
+            emit(s - 2, over[...])
+        if s == COARSE:
+            emit(COARSE - 1, kept[...] + first_over[...])
+        if s >= 5 and s % 2 == 1 and s // 2 - 2 < len(groups) - 2:
             forward(s // 2 - 2)
     for j in range(len(groups) - 2, len(groups)):
         forward(j)
@@ -360,7 +384,7 @@
             pltpu.VMEM((COARSE, FINE * SLOT, DEPTH), bf16),
             pltpu.VMEM((COARSE * rows, FINE * SLOT), f32),
             pltpu.VMEM((FINE * SLOT, COARSE * rows), bf16),
-            pltpu.VMEM((FINE * SLOT, DEPTH), f32),
+            pltpu.VMEM((2, FINE * SLOT, DEPTH), f32),
             pltpu.VMEM((SLOT, DEPTH), f32),
             pltpu.VMEM((SLOT, DEPTH), f32),
             pltpu.VMEM((SLOT, DEPTH), f32),
@@ -389,7 +413,7 @@
     )(
         images,
         pick_counts[None, :],
-        group_of.reshape(parts, rows),
+        group_of[None, :],
         ctf_table,
         precision[None, :],
         references,

time: 69.3 us -> 59.2 us (0.85)
  Pallas kernels: 64.1 us -> 54.1 us
    pallas_call x1, Pallas kernels: 64.1 us -> 54.1 us  [body(): pl.pallas_call(functools.partial(em_kernel, parts, quads), out_shape=[jax...]
    reshape x1 -> x0, local copies, waits for them, and re-layouts: 1.35 us -> none  [body(): group_of.reshape(parts, rows)]
    broadcast_in_dim x0 -> x1, local copies, waits for them, and re-layouts: none -> 1.27 us  [body(): group_of[None, :]]
where the time goes in v3:
time: 59.2 us; the launch traced here: 59 us
  Pallas kernels  54.1 us (91%)
  local copies, waits for them, and re-layouts  4.23 us (7%)
  between operations  0.64 us (1%)
    pallas_call x1, Pallas kernels, body(): pl.pallas_call(functools.partial(em_kernel, parts, quads), out_shape=[jax...  54.1 us
    unnamed x2, local copies, waits for them, and re-layouts  2.97 us
    broadcast_in_dim x1, local copies, waits for them, and re-layouts, body(): group_of[None, :]  1.27 us

profile of v3, /device:TPU:0, one launch (start us, length us, event | category | flops | bytes accessed | tf_op | source)
XLA Modules:
  0.0 59.0 jit_solution(1755970243421168496)
XLA Ops:
  0.6 1.3 %broadcast_in_dim.10.group_rows = s32[1,768]{1,0:T(1,128)} reshape(s32[768]{0:T(1024)} %param.8) | data formatting | bytes 6144 | tf_op jit(solution)/shard_map/broadcast_in_dim | solution.py:416
  1.9 54.1 %em.1 = (f32[50,1728]{1,0:T(8,128)}, f32[1,96]{1,0:T(1,128)}) custom-call(bf16[96,13824]{1,0:T(8,128)(2,1)} %img.1, s32[1,8]{1,0:T(1,128)} %bitcast.3, s32[1,768]{1,0:T(1,128)} %broadcast_in_dim.10.group_rows, f32[32,32]{1,0:T(8,128)} %ctf.1, f32[1,32]{1,0:T(1,128)} %bitcast.4, bf16[50,13824]{1,0:T(8,128)(2,1)} %refs.1), custom_call_target="tpu_custom_call" | custom-call | tf_op jit(solution)/shard_map/em/pallas_call | solution.py:374
  56.0 1.8 %copy.10 = f32[50,1728]{1,0:T(8,128)} copy(f32[50,1728]{1,0:T(8,128)} %get-tuple-element.8) | data formatting | bytes 691200
  57.8 1.2 %copy.11 = f32[96]{0:T(128)} copy(f32[96]{0:T(128)} %bitcast.5) | data formatting | bytes 768

commit v4 on v3

--- a/solution.py
+++ b/solution.py
@@ -292,17 +292,17 @@
     chunk = BUNCH * BLOCK
     place = lax.broadcasted_iota(jnp.int32, (SLOT, chunk), 1) % BLOCK
     for s in range(COARSE + 1):
-
-        @pl.loop(0, DEPTH // chunk)
-        def _(n):
-            columns = pl.ds(pl.multiple_of(n * chunk, 128), chunk)
+        for n in range(DEPTH // chunk):
+            columns = slice(n * chunk, (n + 1) * chunk)
             if s > 0:
-                old = fresh.at[(s - 1) % 2]
-                stay = old[:SLOT, columns]
+                old = (s - 1) % 2
+                stay = fresh[old, :SLOT, columns]
                 beyond = jnp.zeros((SLOT, chunk), f32)
                 for turn in range(1, FINE):
                     moved = pltpu.roll(
-                        old[turn * SLOT : (turn + 1) * SLOT, columns], chunk - turn * TURN, 1
+                        fresh[old, turn * SLOT : (turn + 1) * SLOT, columns],
+                        chunk - turn * TURN,
+                        1,
                     )
                     inside = place < BLOCK - turn * TURN
                     stay = stay + jnp.where(inside, moved, 0.0)

time: 59.2 us -> 64.2 us (1.084)
  Pallas kernels: 54.1 us -> 59.1 us
    pallas_call x1, Pallas kernels: 54.1 us -> 59.1 us  [body(): pl.pallas_call(functools.partial(em_kernel, parts, quads), out_shape=[jax...]
where the time goes in v4:
time: 64.2 us; the launch traced here: 64 us
  Pallas kernels  59.1 us (92%)
  local copies, waits for them, and re-layouts  4.23 us (7%)
    pallas_call x1, Pallas kernels, body(): pl.pallas_call(functools.partial(em_kernel, parts, quads), out_shape=[jax...  59.1 us
    unnamed x2, local copies, waits for them, and re-layouts  2.97 us

profile of v4, /device:TPU:0, one launch (start us, length us, event | category | flops | bytes accessed | tf_op | source)
XLA Modules:
  0.0 64.0 jit_solution(4311291596255125827)
XLA Ops:
  0.6 1.3 %broadcast_in_dim.10.group_rows = s32[1,768]{1,0:T(1,128)} reshape(s32[768]{0:T(1024)} %param.8) | data formatting | bytes 6144 | tf_op jit(solution)/shard_map/broadcast_in_dim | solution.py:416
  1.9 59.1 %em.1 = (f32[50,1728]{1,0:T(8,128)}, f32[1,96]{1,0:T(1,128)}) custom-call(bf16[96,13824]{1,0:T(8,128)(2,1)} %img.1, s32[1,8]{1,0:T(1,128)} %bitcast.3, s32[1,768]{1,0:T(1,128)} %broadcast_in_dim.10.group_rows, f32[32,32]{1,0:T(8,128)} %ctf.1, f32[1,32]{1,0:T(1,128)} %bitcast.4, bf16[50,13824]{1,0:T(8,128)(2,1)} %refs.1), custom_call_target="tpu_custom_call" | custom-call | tf_op jit(solution)/shard_map/em/pallas_call | solution.py:374
  61.0 1.8 %copy.10 = f32[50,1728]{1,0:T(8,128)} copy(f32[50,1728]{1,0:T(8,128)} %get-tuple-element.8) | data formatting | bytes 691200
  62.8 1.2 %copy.11 = f32[96]{0:T(128)} copy(f32[96]{0:T(128)} %bitcast.5) | data formatting | bytes 768
